TPU v7x, 32 devices: a whole 2x2x4 slice. The times are simulated.
32 devices in a mesh: slides: 2 (over x), cols: 8 (over z, y), rows: 2 (over core).
Axes of the slice: x: 2, y: 2, z: 4, core: 2. Of those that a mesh axis runs over, the one named last changes fastest.
Arguments:
- pixels: bfloat16 [3, 256, 8192], P(None, 'rows', ('slides', 'cols')), parts along dimension 2, may hold values from -6 to 6
- patch_weight: bfloat16 [24, 24, 3, 768], replicated, may hold values from -0.15625 to 0.15625
- patch_bias: float32 [768], replicated, may hold values from -3 to 3
- norm_gain: float32 [768], replicated, may hold values from 0.1 to 1.9
- gate_weight: bfloat16 [768, 1536], replicated, may hold values from -0.21875 to 0.21875
- mix_weight: bfloat16 [768, 1664], replicated, may hold values from -0.21875 to 0.21875
- step_weight: bfloat16 [768, 24], replicated, may hold values from -0.21875 to 0.21875
- step_bias: float32 [24], replicated, may hold values from -5 to -2
- log_rate: float32 [24], replicated, may hold values from -11 to 2
- conv_weight: float32 [4, 1664], replicated, may hold values from -3 to 3
- conv_bias: float32 [1664], replicated, may hold values from -3 to 3
- skip_gain: float32 [24], replicated, may hold values from 0.25 to 2
- out_gain: float32 [1536], replicated, may hold values from 0.1 to 1.9
- out_weight: bfloat16 [1536, 768], replicated, may hold values from -0.15625 to 0.15625
Outputs:
- layer_out: bfloat16 [8192, 768], P(('slides', 'cols', 'rows')), parts along dimension 0
There are 2 independent parts, one for each index of `slides`. A program takes and returns all parts, laid end to end along the dimension named above; an argument that names none is the same for every part. Nothing has to cross between parts.
All inputs are finite; a program needn't handle non-finite values.
Results may differ from a plain program's by a relative error of at most 0.011.
Values may be sent and summed in bfloat16 or wider, within the bound.
A program may use at most 192 MiB of HBM per device.

v0:
```python
import jax
import jax.numpy as jnp
from jax import lax
from jax.sharding import PartitionSpec as P

E = 1536
HDIM = 64
NSTATE = 64
PATCH = 16
KERNEL = 24
SPAN = 256
HEADS = 24


def extended(block, sides, width):
    for axis, dim in sides:
        count = lax.axis_size(axis)
        forward = [(i, i + 1) for i in range(count - 1)]
        backward = [(target, source) for source, target in forward]
        low = lax.ppermute(
            lax.slice_in_dim(block, block.shape[dim] - width, None, axis=dim), axis, forward
        )
        high = lax.ppermute(lax.slice_in_dim(block, 0, width, axis=dim), axis, backward)
        block = jnp.concatenate([low, block, high], axis=dim)
    return block


def shifted(block, axis, distance):
    devices = range(lax.axis_size(axis))
    route = [(i - distance, i) for i in devices if i - distance in devices]
    return lax.ppermute(block, axis, route)


def from_partner(block, axis, distance):
    count = lax.axis_size(axis)
    route = []
    for low in range(count):
        high = low | 1 << distance
        if high != low and high < count:
            route += [(low, high), (high, low)]
    return lax.ppermute(block, axis, route)


def carried_in(shard, axis, join, neutral):
    place = lax.axis_index(axis)
    gathered = jax.tree.map(
        lambda a, kind: lax.all_gather(a.astype(kind), axis),
        shard,
        jax.tree.map(lambda a: jnp.bfloat16 if a.dtype == jnp.float32 else a.dtype, shard),
    )
    state = jax.tree.map(lambda a, e: jnp.zeros_like(a) + jnp.asarray(e, a.dtype), shard, neutral)

    def one(lap, state):
        return join(
            state,
            jax.tree.map(
                lambda a, own: lax.dynamic_index_in_dim(a, lap, 0, False).astype(own.dtype),
                gathered,
                shard,
            ),
        )

    return lax.fori_loop(0, place, one, state)


def rms_scale(values, gains):
    mean_sq = jnp.mean(values * values, axis=-1, keepdims=True)
    return values * lax.rsqrt(mean_sq + 1e-05) * gains


def combine_states(earlier, latter):
    decay_first, state_first = earlier
    decay_second, state_second = latter
    return (decay_first * decay_second, decay_second[:, None, None] * state_first + state_second)


def body(
    pixels,
    patch_weight,
    patch_bias,
    norm_gain,
    gate_weight,
    mix_weight,
    step_weight,
    step_bias,
    log_rate,
    conv_weight,
    conv_bias,
    skip_gain,
    out_gain,
    out_weight,
):
    margin = (KERNEL - PATCH) // 2
    padded = extended(pixels, (("cols", 2), ("rows", 1)), margin)
    embed_grid = lax.conv_general_dilated(
        padded[None],
        patch_weight,
        (PATCH, PATCH),
        "VALID",
        dimension_numbers=("NCHW", "HWIO", "NHWC"),
        preferred_element_type=jnp.float32,
    )[0]
    embed_grid = (embed_grid + patch_bias).astype(jnp.bfloat16)
    row_local, col_local, feature_width = embed_grid.shape
    devices = lax.axis_size(("cols", "rows"))
    row_count = lax.axis_size("rows")
    col_count = lax.axis_size("cols")
    groups = col_count // row_local
    piece_len = col_local * feature_width // devices
    outgoing = embed_grid.reshape(row_local, devices, piece_len)
    spread = lax.all_to_all(outgoing, ("cols", "rows"), split_axis=1, concat_axis=1, tiled=True)
    spread = spread.reshape(row_local, groups, row_local, row_count, piece_len).transpose(
        3, 0, 1, 2, 4
    )
    landed = lax.all_to_all(
        spread.reshape(devices, row_local, piece_len),
        ("cols", "rows"),
        split_axis=0,
        concat_axis=0,
        tiled=True,
    )
    tokens = landed.transpose(1, 0, 2).reshape(row_local * col_local, feature_width)
    resid = tokens.astype(jnp.float32)
    normed = rms_scale(resid, norm_gain).astype(jnp.bfloat16)
    gate_proj = jnp.dot(normed, gate_weight, preferred_element_type=jnp.float32).astype(
        jnp.bfloat16
    )
    mixed_raw = jnp.dot(normed, mix_weight, preferred_element_type=jnp.float32).astype(jnp.bfloat16)
    step_raw = jnp.dot(normed, step_weight, preferred_element_type=jnp.float32)
    length = mixed_raw.shape[0]
    taps = conv_weight.shape[0]
    tail = shifted(mixed_raw[length - (taps - 1) :], ("cols", "rows"), 1)
    window = jnp.concatenate([tail, mixed_raw], 0).astype(jnp.float32)
    conv_sum = conv_bias
    for offset in range(taps):
        conv_sum = conv_sum + conv_weight[offset] * window[offset : offset + length]
    mixed = jax.nn.silu(conv_sum).astype(jnp.bfloat16)
    step_size = jax.nn.softplus(step_raw + step_bias)
    log_decay = -step_size * jnp.exp(log_rate)
    blocks = length // SPAN
    head_in = mixed[:, :E].reshape(blocks, SPAN, HEADS, HDIM)
    b_mat = mixed[:, E : E + NSTATE].reshape(blocks, SPAN, NSTATE)
    c_mat = mixed[:, E + NSTATE :].reshape(blocks, SPAN, NSTATE)
    step_blocks = step_size.reshape(blocks, SPAN, HEADS)
    cum_decay = jnp.cumsum(log_decay.reshape(blocks, SPAN, HEADS), axis=1)
    scores = jnp.einsum("ctn,csn->cts", c_mat, b_mat, preferred_element_type=jnp.float32)
    cum_heads = cum_decay.transpose(0, 2, 1)
    decay_gap = cum_heads[:, :, :, None] - cum_heads[:, :, None, :]
    causal = lax.broadcasted_iota(jnp.int32, (SPAN, SPAN), 0) >= lax.broadcasted_iota(
        jnp.int32, (SPAN, SPAN), 1
    )
    decay_w = jnp.where(causal, jnp.exp(jnp.where(causal, decay_gap, 0.0)), 0.0)
    weights = (scores[:, None] * decay_w * step_blocks.transpose(0, 2, 1)[:, :, None, :]).astype(
        jnp.bfloat16
    )
    y_intra = jnp.einsum("chts,cshp->cthp", weights, head_in, preferred_element_type=jnp.float32)
    inputs_f = head_in.astype(jnp.float32)
    to_end = jnp.exp(cum_decay[:, -1:] - cum_decay) * step_blocks
    fresh_state = jnp.einsum(
        "cthp,ctn->chpn",
        inputs_f * to_end[..., None],
        b_mat.astype(jnp.float32),
        precision=lax.Precision.HIGHEST,
    )
    block_decay = jnp.exp(cum_decay[:, -1])
    local_states = []
    prefix_decay = []
    running = jnp.zeros((HEADS, HDIM, NSTATE), jnp.float32)
    total_decay = jnp.ones((HEADS,), jnp.float32)
    for index in range(blocks):
        local_states.append(running)
        prefix_decay.append(total_decay)
        running = block_decay[index][:, None, None] * running + fresh_state[index]
        total_decay = total_decay * block_decay[index]
    summary = (total_decay, running)
    identity = (jnp.ones_like(total_decay), jnp.zeros_like(running))
    partner = (
        from_partner(summary[0].astype(jnp.bfloat16), "rows", 0).astype(jnp.float32),
        from_partner(summary[1].astype(jnp.bfloat16), "rows", 0).astype(jnp.float32),
    )
    upper_row = lax.axis_index("rows") == 1
    lower_part = (
        jnp.where(upper_row, partner[0], summary[0]),
        jnp.where(upper_row, partner[1], summary[1]),
    )
    upper_part = (
        jnp.where(upper_row, summary[0], partner[0]),
        jnp.where(upper_row, summary[1], partner[1]),
    )
    pair_total = combine_states(lower_part, upper_part)
    before = carried_in(pair_total, "cols", combine_states, identity)
    joined_lower = combine_states(before, lower_part)
    incoming = jnp.where(upper_row, joined_lower[1], before[1])
    block_states = jnp.stack(
        [
            prefix_decay[index][:, None, None] * incoming + local_states[index]
            for index in range(blocks)
        ]
    )
    y_state = jnp.exp(cum_decay)[..., None] * jnp.einsum(
        "chpn,ctn->cthp", block_states, c_mat.astype(jnp.float32), precision=lax.Precision.HIGHEST
    )
    head_out = y_intra + y_state + skip_gain[None, None, :, None] * inputs_f
    gated = head_out.reshape(length, E) * jax.nn.silu(gate_proj.astype(jnp.float32))
    hidden = rms_scale(gated, out_gain).astype(jnp.bfloat16)
    return (jnp.dot(hidden, out_weight, preferred_element_type=jnp.float32) + resid).astype(
        jnp.bfloat16
    )


def solution(mesh):
    placed = (
        P(None, "rows", ("slides", "cols")),
        P(),
        P(),
        P(),
        P(),
        P(),
        P(),
        P(),
        P(),
        P(),
        P(),
        P(),
        P(),
        P(),
    )
    return jax.shard_map(
        body,
        mesh=mesh,
        in_specs=placed,
        out_specs=P(("slides", "cols", "rows"), None),
        check_vma=False,
    )
```

profile of v0, /device:TPU:28, one launch (start us, length us, event | category | flops | bytes accessed | tf_op | source)
XLA Modules:
  0.0 241.1 jit_solution(2868747071850368426)
XLA Ops:
  7.7 1.3 collective-permute-start
  9.0 4.6 %collective-permute-start.1 = (bf16[3,128,4]{2,1,0:T(8,128)(2,1)S(1)}, bf16[3,128,4]{2,1,0:T(8,128)(2,1)S(1)}, u32[]{:S(2)}, u32[]{:S(2)}) collective-permute-start(bf16[3,128,4]{2,1,0:T(8,128)(2,1)S(1)} %get-tuple-element.74), channel_id=1, source_target_pairs={{2,0},{4,2},{6,4},{8,6},{10,8},{12,10},{14,12},{3,1},{5,3},{7,5},{... | collective-permute-start | bytes 9224 | tf_op jit(solution)/shard_map/ppermute | solution.py:23
  14.2 1.5 collective-permute-done.1
  21.0 1.4 maximum_bitcast_fusion
  23.3 2.0 reshape.217
  25.3 10.1 %copy.64 = bf16[3,136,1,8,80]{3,0,4,1,2:T(4,128)(2,1)} copy(bf16[3,136,1,8,80]{4,3,1,0,2:T(8,128)(2,1)S(1)} %reshape.217) | data formatting | bytes 1044480 | tf_op jit(solution)/shard_map/conv_general_dilated | solution.py:95
  35.4 3.7 %slice.79 = bf16[3,136,1,7,23]{3,0,4,1,2:T(4,128)(2,1)S(1)} slice(bf16[3,136,1,8,80]{3,0,4,1,2:T(4,128)(2,1)} %copy.64), slice={[0:3], [0:136], [0:1], [1:8], [0:23]} | slice | bytes 262752 | tf_op jit(solution)/shard_map/conv_general_dilated | solution.py:95
  39.1 40.8 %fusion.20 = f32[8,8,5,768]{3,1,2,0:T(8,128)S(1)} fusion(bf16[24,24,3,768]{3,1,2,0:T(8,128)(2,1)S(1)} %copy-done, bf16[3,136,1,7,23]{3,0,4,1,2:T(4,128)(2,1)S(1)} %slice.79, bf16[3,136,1,8,80]{3,0,4,1,2:T(4,128)(2,1)} %copy.64, pred[8,5]{0,1:T(8,128)(4,1)S(1)} %copy-done.27), kind=kOutput, calls=%fused_computation.34 | convolution fusion | flops 851609472 | bytes 4290904 | tf_op jit(solution)/shard_map/conv_general_dilated | solution.py:95
  81.4 1.4 squeeze.14
  83.1 17.3 %all_to_all.10 = bf16[8,16,1536]{2,0,1:T(8,128)(2,1)S(1)} all-to-all(bf16[8,16,1536]{2,0,1:T(8,128)(2,1)S(1)} %copy.68), channel_id=1, replica_groups=mesh['slides'=2,'cols'=8,'rows'=2] {'cols','rows'}, dimensions={1} | all-to-all | bytes 786432 | tf_op jit(solution)/shard_map/all_to_all | solution.py:111
  101.4 6.0 %all-to-all-start.1 = ((bf16[16,8,1536]{2,1,0:T(8,128)(2,1)}), bf16[16,8,1536]{2,1,0:T(8,128)(2,1)S(1)}, u32[]{:S(2)}, u32[]{:S(2)}) async-start(bf16[16,8,1536]{2,1,0:T(8,128)(2,1)} %bitcast.7), calls=%async_computation.1 | async-start | bytes 786432 | tf_op jit(solution)/shard_map/all_to_all | solution.py:115
  108.2 9.0 %all-to-all-done.1 = bf16[16,8,1536]{2,1,0:T(8,128)(2,1)S(1)} async-done(((bf16[16,8,1536]{2,1,0:T(8,128)(2,1)}), bf16[16,8,1536]{2,1,0:T(8,128)(2,1)S(1)}, u32[]{:S(2)}, u32[]{:S(2)}) %all-to-all-start.1) | async-done | bytes 393248 | tf_op jit(solution)/shard_map/all_to_all | solution.py:115
  117.2 1.4 copy.70
  122.8 1.4 exponential_bitcast_fusion
  125.8 3.1 %copy.76 = f32[256,1536]{1,0:T(8,128)} copy(f32[256,1536]{0,1:T(8,128)} %bitcast.106) | data formatting | bytes 3145728 | tf_op jit(solution)/shard_map/mul | solution.py:161
  128.9 2.6 %convolution_convert_fusion.1 = bf16[256,1664]{1,0:T(8,128)(2,1)S(1)} fusion(bf16[256,768]{1,0:T(8,128)(2,1)S(1)} %copy-done.9, bf16[768,1664]{1,0:T(8,128)(2,1)} %param.21), kind=kOutput, calls=%fused_computation.18 | convolution fusion | flops 654737408 | bytes 3801088 | tf_op jit(solution)/shard_map/dot_general | solution.py:128
  131.6 2.2 collective-permute-start.4
  138.2 1.4 convert_multiply_fusion
  139.6 3.1 %copy.77 = f32[256,1536]{0,1:T(8,128)} copy(f32[256,1536]{1,0:T(8,128)} %convert_multiply_fusion) | data formatting | bytes 3145728 | tf_op jit(solution)/shard_map/mul | solution.py:161
  142.7 2.2 fusion.50
  145.0 1.7 collective-permute-done.6
  153.4 17.7 %all-reduce = bf16[192]{0:T(256)(128)(2,1)} all-reduce(bf16[192]{0:T(256)(128)(2,1)} %dynamic-update-slice), channel_id=2, replica_groups=mesh['slides'=2,'cols'=8,'rows'=2] {'cols'}, use_global_device_ids=true, to_apply=%add | all-reduce | flops 192 | bytes 768
  172.3 1.7 slice_convert_fusion
  174.0 2.3 copy.71
  176.3 3.0 %copy.80 = f32[256,1536]{0,1:T(8,128)} copy(f32[256,1536]{1,0:T(8,128)} %get-tuple-element.69) | data formatting | bytes 3145728 | tf_op jit(solution)/shard_map/convert_element_type | solution.py:157
  179.6 4.6 %fusion.7 = f32[24,64,256]{2,1,0:T(8,128)} fusion(bf16[256,24,64]{0,2,1:T(8,128)(2,1)} %bitcast.112, f32[24,256]{1,0:T(8,128)S(1)} %bitcast.113, f32[24,256]{1,0:T(8,128)S(1)} %bitcast_add_fusion.1, f32[256,256]{1,0:T(8,128)S(1)} %fusion.38, pred[256,256]{1,0:T(8,128)(4,1)} %iota_compare_fusion.1), kind=kOutput, calls=%fused_computation.10 | convolution fusion | flops 210763776 | bytes 2736128 | tf_op jit(solution)/shard_map/chts,cshp->cthp/dot_general | solution.py:156
  184.2 24.2 %all-gather.4.cloned.1.call-done = bf16[192,64,64]{2,1,0:T(8,128)(2,1)} async-done(((bf16[24,64,64]{2,1,0:T(8,128)(2,1)}), bf16[192,64,64]{2,1,0:T(8,128)(2,1)}) %all-gather.4.cloned.1.call-update) | async-done | bytes 1572880 | tf_op jit(solution)/shard_map/all_gather | solution.py:47
  208.5 13.3 %while.12 = (s32[]{:T(128)}, f32[24,64,64]{2,1,0:T(8,128)S(1)}, s32[]{:T(128)}, bf16[8,24]{1,0:T(8,128)(2,1)}, bf16[8,24,64,64]{3,2,1,0:T(8,128)(2,1)}, /*index=5*/s32[]{:T(128)}, s32[]{:T(128)}, s32[]{:T(128)}) while((s32[]{:T(128)}, f32[24,64,64]{2,1,0:T(8,128)S(1)}, s32[]{:T(128)}, bf16[8,24]{1,0:T(8,128)(2,1)}, ...), condition=%wide.region_4.5_spmd, body=%wide.region_3.4_spmd.sunk | while | flops 294941 | bytes 983407 | solution.py:63
  221.8 4.4 %fusion.19 = f32[1,256,24,64]{1,3,2,0:T(8,128)} fusion(f32[24,64,256]{2,1,0:T(8,128)} %fusion.7, f32[1,256,24,64]{1,3,2,0:T(8,128)} %bitcast.107, f32[24]{0:T(128)S(1)} %copy-done.24, f32[24,64,64]{2,1,0:T(8,128)S(1)} %get-tuple-element.49, f32[256,24]{0,1:T(8,128)S(1)} %copy-done.12, f32[24,64,64]{2,1,0:T(8,128)} %copy-done.4, ...), kind=kOutput, calls=%fused_computation.30 | convolution fusion | flops 304054272 | bytes 6381761 | tf_op jit(solution)/shard_map/chpn,ctn->cthp/dot_general | solution.py:200
  226.2 3.1 %copy.81 = f32[256,1536]{1,0:T(8,128)} copy(f32[256,1536]{0,1:T(8,128)} %bitcast.108) | data formatting | bytes 3145728 | tf_op jit(solution)/shard_map/reshape | solution.py:204
  229.3 3.3 %multiply_reduce_fusion = (f32[256]{0:T(256)S(1)}, f32[256,1536]{1,0:T(8,128)S(1)}) fusion(f32[256,1536]{1,0:T(8,128)} %copy.81, bf16[256,768]{1,0:T(8,128)(2,1)S(1)} %copy-done.10, bf16[768,1536]{1,0:T(8,128)(2,1)} %param.20), kind=kOutput, calls=%fused_computation.32 | convolution fusion | flops 607518464 | bytes 5899264 | tf_op jit(solution)/shard_map/dot_general | solution.py:125
  232.6 1.6 fusion.25
  (127 shorter events, 42.1 us)
Async XLA Ops:
  6.5 32.5 %copy-start = (bf16[24,24,3,768]{3,1,2,0:T(8,128)(2,1)S(1)}, bf16[24,24,3,768]{3,1,2,0:T(8,128)(2,1)}, u32[]{:S(2)}) copy-start(bf16[24,24,3,768]{3,1,2,0:T(8,128)(2,1)} %param.17) | copy-start | bytes 7962628
  7.7 6.5 %collective-permute-start = (bf16[3,128,4]{2,1,0:T(8,128)(2,1)S(1)}, bf16[3,128,4]{2,1,0:T(8,128)(2,1)S(1)}, u32[]{:S(2)}, u32[]{:S(2)}) collective-permute-start(bf16[3,128,4]{2,1,0:T(8,128)(2,1)S(1)} %get-tuple-element.73), channel_id=1, source_target_pairs={{0,2},{2,4},{4,6},{6,8},{8,10},{10,12},{12,14},{1,3},{3,5},{5,7},{... | collective-permute-start | bytes 9224 | tf_op jit(solution)/shard_map/ppermute | solution.py:20
  9.0 6.8 %collective-permute-start.1 = (bf16[3,128,4]{2,1,0:T(8,128)(2,1)S(1)}, bf16[3,128,4]{2,1,0:T(8,128)(2,1)S(1)}, u32[]{:S(2)}, u32[]{:S(2)}) collective-permute-start(bf16[3,128,4]{2,1,0:T(8,128)(2,1)S(1)} %get-tuple-element.74), channel_id=1, source_target_pairs={{2,0},{4,2},{6,4},{8,6},{10,8},{12,10},{14,12},{3,1},{5,3},{7,5},{... | collective-permute-start | bytes 9224 | tf_op jit(solution)/shard_map/ppermute | solution.py:23
  16.6 3.3 %collective-permute-start.2 = (bf16[3,4,520]{2,1,0:T(4,128)(2,1)S(1)}, bf16[3,4,520]{2,1,0:T(4,128)(2,1)S(1)}, u32[]{:S(2)}, u32[]{:S(2)}) collective-permute-start(bf16[3,4,520]{2,1,0:T(4,128)(2,1)S(1)} %get-tuple-element.71), channel_id=1, source_target_pairs={{0,1},{2,3},{4,5},{6,7},{8,9},{10,11},{12,13},{14,15},{16,17},{18,... | collective-permute-start | bytes 37448 | tf_op jit(solution)/shard_map/ppermute | solution.py:20
  17.9 3.1 %collective-permute-start.3 = (bf16[3,4,520]{2,1,0:T(4,128)(2,1)S(1)}, bf16[3,4,520]{2,1,0:T(4,128)(2,1)S(1)}, u32[]{:S(2)}, u32[]{:S(2)}) collective-permute-start(bf16[3,4,520]{2,1,0:T(4,128)(2,1)S(1)} %get-tuple-element.72), channel_id=1, source_target_pairs={{1,0},{3,2},{5,4},{7,6},{9,8},{11,10},{13,12},{15,14},{17,16},{19,... | collective-permute-start | bytes 37448 | tf_op jit(solution)/shard_map/ppermute | solution.py:23
  35.4 3.7 %copy-start.27 = (pred[8,5]{0,1:T(8,128)(4,1)S(1)}, pred[8,5]{0,1:T(8,128)(4,1)}, u32[]{:S(2)}) copy-start(pred[8,5]{0,1:T(8,128)(4,1)} %constant.53) | copy-start | bytes 124
  82.9 24.6 %copy-start.26 = (f32[24]{0:T(128)S(1)}, f32[24]{0:T(128)}, u32[]{:S(2)}) copy-start(f32[24]{0:T(128)} %param.24) | copy-start | bytes 292
  82.9 24.6 %copy-start.19 = (f32[4,1664]{1,0:T(4,128)S(1)}, f32[4,1664]{1,0:T(4,128)}, u32[]{:S(2)}) copy-start(f32[4,1664]{1,0:T(4,128)} %param.25) | copy-start | bytes 79876
  101.4 15.7 %all-to-all-start.1 = ((bf16[16,8,1536]{2,1,0:T(8,128)(2,1)}), bf16[16,8,1536]{2,1,0:T(8,128)(2,1)S(1)}, u32[]{:S(2)}, u32[]{:S(2)}) async-start(bf16[16,8,1536]{2,1,0:T(8,128)(2,1)} %bitcast.7), calls=%async_computation.1 | async-start | bytes 786432 | tf_op jit(solution)/shard_map/all_to_all | solution.py:115
  107.4 100.9 %all-gather.4.cloned.1.call-start = ((), (), s32[]{:S(2)}) async-start(), calls=%async_computation.2 | async-start | bytes 3538944 | tf_op jit(solution)/shard_map/all_gather | solution.py:47
  117.2 2.8 %copy-start.21 = (f32[768]{0:T(1024)S(1)}, f32[768]{0:T(1024)}, u32[]{:S(2)}) copy-start(f32[768]{0:T(1024)} %param.19) | copy-start | bytes 9220
  118.6 2.3 copy-start.25
  119.8 5.9 %copy-start.1 = (f32[256,768]{1,0:T(8,128)}, f32[256,768]{1,0:T(8,128)S(1)}, u32[]{:S(2)}) copy-start(f32[256,768]{1,0:T(8,128)S(1)} %reshape.224) | copy-start | bytes 2359300
  122.2 6.7 %copy-start.11 = (f32[24,2,128]{2,1,0:T(2,128)}, f32[24,2,128]{2,1,0:T(2,128)S(1)}, u32[]{:S(2)}) copy-start(f32[24,2,128]{2,1,0:T(2,128)S(1)} %broadcast.108) | copy-start | bytes 73732
  125.8 3.1 %copy-start.9 = (bf16[256,768]{1,0:T(8,128)(2,1)S(1)}, bf16[256,768]{1,0:T(8,128)(2,1)}, u32[]{:S(2)}) copy-start(bf16[256,768]{1,0:T(8,128)(2,1)} %copy-done.8) | copy-start | bytes 1179652
  131.5 5.3 %copy-start.15 = (f32[1664]{0:T(1024)S(1)}, f32[1664]{0:T(1024)}, u32[]{:S(2)}) copy-start(f32[1664]{0:T(1024)} %get-tuple-element.50) | copy-start | bytes 19972
  131.5 5.3 %copy-start.16 = (f32[1664]{0:T(1024)S(1)}, f32[1664]{0:T(1024)}, u32[]{:S(2)}) copy-start(f32[1664]{0:T(1024)} %get-tuple-element.51) | copy-start | bytes 19972
  131.5 5.3 %copy-start.17 = (f32[1664]{0:T(1024)S(1)}, f32[1664]{0:T(1024)}, u32[]{:S(2)}) copy-start(f32[1664]{0:T(1024)} %get-tuple-element.52) | copy-start | bytes 19972
  131.5 5.3 %copy-start.18 = (f32[1664]{0:T(1024)S(1)}, f32[1664]{0:T(1024)}, u32[]{:S(2)}) copy-start(f32[1664]{0:T(1024)} %get-tuple-element.53) | copy-start | bytes 19972
  131.5 5.3 %copy-start.20 = (f32[1664]{0:T(1024)S(1)}, f32[1664]{0:T(1024)}, u32[]{:S(2)}) copy-start(f32[1664]{0:T(1024)} %param.26) | copy-start | bytes 19972
  131.6 5.0 %collective-permute-start.4 = (bf16[3,1664]{1,0:T(4,128)(2,1)S(1)}, bf16[3,1664]{1,0:T(4,128)(2,1)S(1)}, u32[]{:S(2)}, u32[]{:S(2)}) collective-permute-start(bf16[3,1664]{1,0:T(4,128)(2,1)S(1)} %slice.81), channel_id=1, source_target_pairs={{0,1},{1,2},{2,3},{3,4},{4,5},{5,6},{6,7},{7,8},{8,9},{9,10},{10,1... | collective-permute-start | bytes 29960 | tf_op jit(solution)/shard_map/ppermute | solution.py:31
  133.8 1.2 collective-permute-start.5
  138.2 41.2 %copy-start.3 = (bf16[256,1664]{1,0:T(8,128)(2,1)}, bf16[256,1664]{1,0:T(8,128)(2,1)S(1)}, u32[]{:S(2)}) copy-start(bf16[256,1664]{1,0:T(8,128)(2,1)S(1)} %multiply_convert_fusion.2) | copy-start | bytes 2555908
  142.7 4.8 %copy-start.23 = (f32[24]{0:T(128)S(1)}, f32[24]{0:T(128)}, u32[]{:S(2)}) copy-start(f32[24]{0:T(128)} %get-tuple-element.67) | copy-start | bytes 292
  144.9 1.8 collective-permute-start.6
  208.4 13.3 %copy-start.12 = (f32[256,24]{0,1:T(8,128)S(1)}, f32[256,24]{0,1:T(8,128)}, u32[]{:S(2)}) copy-start(f32[256,24]{0,1:T(8,128)} %get-tuple-element.64) | copy-start | bytes 73732
  208.4 13.3 %copy-start.22 = (f32[24]{0:T(128)S(1)}, f32[24]{0:T(128)}, u32[]{:S(2)}) copy-start(f32[24]{0:T(128)} %get-tuple-element.68) | copy-start | bytes 292
  208.4 13.3 %copy-start.24 = (f32[24]{0:T(128)S(1)}, f32[24]{0:T(128)}, u32[]{:S(2)}) copy-start(f32[24]{0:T(128)} %param.27) | copy-start | bytes 292
  226.2 3.1 %copy-start.10 = (bf16[256,768]{1,0:T(8,128)(2,1)S(1)}, bf16[256,768]{1,0:T(8,128)(2,1)}, u32[]{:S(2)}) copy-start(bf16[256,768]{1,0:T(8,128)(2,1)} %copy-done.8) | copy-start | bytes 1179652
  229.3 3.3 %copy-start.2 = (f32[256,768]{1,0:T(8,128)S(1)}, f32[256,768]{1,0:T(8,128)}, u32[]{:S(2)}) copy-start(f32[256,768]{1,0:T(8,128)} %copy-done.1) | copy-start | bytes 2359300
  229.3 3.3 %copy-start.6 = (bf16[1536,768]{1,0:T(8,128)(2,1)S(1)}, bf16[1536,768]{1,0:T(8,128)(2,1)}, u32[]{:S(2)}) copy-start(bf16[1536,768]{1,0:T(8,128)(2,1)} %param.29) | copy-start | bytes 7077892
  229.3 3.3 %copy-start.14 = (f32[1536]{0:T(1024)S(1)}, f32[1536]{0:T(1024)}, u32[]{:S(2)}) copy-start(f32[1536]{0:T(1024)} %param.28) | copy-start | bytes 18436
  (5 other events, 7.1 us)
Sparse Core Ops, SparseCore 0:
  148.6 59.7 all-gather.3
where the time goes:
time: 243 us; the launch traced here: 241 us
  matrix products  60 us (25%)
  local copies, waits for them, and re-layouts  49.2 us (20%)
  waiting for transfers between devices  40.2 us (17%)
  blocking collectives  35 us (14%)
  other arithmetic  24.8 us (10%)
  starting transfers between devices  16.8 us (7%)
  between operations  14.6 us (6%)
    conv_general_dilated x1, matrix products, body(): lax.conv_general_dilated(padded[None], patch_weight, (PATCH, PATCH), 'VAL...  40.8 us
    all_gather x1, waiting for transfers between devices, carried_in(): lax.all_gather(a.astype(kind), axis)  24.2 us
    unnamed x1, blocking collectives  17.7 us
    conv_general_dilated x6, local copies, waits for them, and re-layouts, body(): lax.conv_general_dilated(padded[None], patch_weight, (PATCH, PATCH), 'VAL...  17.3 us
    all_to_all x1, blocking collectives, body(): lax.all_to_all(outgoing, ('cols', 'rows'), split_axis=1, concat_axis=1, t...  17.3 us
    all_to_all x1, waiting for transfers between devices, body(): lax.all_to_all(spread.reshape(devices, row_local, piece_len), ('cols', 'r...  8.95 us
    add x7, other arithmetic, combine_states(): decay_second[:, None, None] * state_first + state_second  8.38 us
    mul x3, local copies, waits for them, and re-layouts, body(): inputs_f * to_end[..., None]  7.43 us
  transfers between devices with their start and end apart: 9, of which 8 were waited for; matrix products, arithmetic and copies ran while one was open for 8% of the time, Pallas kernels for 0%

commit v1 on v0

v1 whole, which is shorter than its diff:
```python
import functools

import jax
import jax.numpy as jnp
from jax import lax
from jax.experimental import pallas as pl
from jax.experimental.pallas import tpu as pltpu
from jax.sharding import PartitionSpec as P

E = 1536
HDIM = 64
NSTATE = 64
PATCH = 16
KERNEL = 24
SPAN = 256
HEADS = 24


F32 = jnp.float32
BF16 = jnp.bfloat16
CHAN = 3
LEAD = 16
WIN = 80
OWN_AT = 16 + 256 + 16
HI = lax.Precision.HIGHEST


def layer_kernel(
    dims, x_ref, wp_hbm, mix_hbm, gate_hbm, out_hbm, step_ref, small_ref, o_ref,
    wp, mixw, gatew, outw, w_sem,
    recv, recv_prev, recv_next, trans, patches, emb, normed, raw, mixed, gate, yacc, xw,
    squart, squart_in, logs, tot_out, tot_in, inc_out, inc_in, inc_acc,
    x_send, x_prev_send, x_next_send, x_recv, prev_recv, next_recv,
    q_send, q_recv, l_send, l_recv, t_send, t_recv, i_send, i_recv,
):
    cols, nr, local_rows, width = dims
    ndev = cols * nr
    parts = ndev // (local_rows * nr)
    per_part = cols // parts
    ngroup = ndev // 4
    d_model = emb.shape[1]
    c = lax.axis_index("cols")
    r = lax.axis_index("rows")
    me = c * nr + r
    e = lax.rem(me, 4)
    g = me // 4

    def dev(index):
        return {"cols": index // nr, "rows": lax.rem(index, nr)}

    loads = [
        pltpu.make_async_copy(s, t, w_sem.at[n])
        for n, (s, t) in enumerate(
            ((wp_hbm, wp), (mix_hbm, mixw), (gate_hbm, gatew), (out_hbm, outw))
        )
    ]
    for load in loads:
        load.start()

    barrier = pltpu.get_barrier_semaphore()
    for hop in range(1, ndev):
        pl.semaphore_signal(
            barrier, inc=1, device_id=dev(lax.rem(me + hop, ndev)),
            device_id_type=pl.DeviceIdType.MESH,
        )
    pl.semaphore_wait(barrier, ndev - 1)

    def push(cond, src, dst, send, recv_s, target):
        away = cond & (target != me)
        own = cond & (target == me)

        def remote():
            return pltpu.make_async_remote_copy(
                src, dst, send, recv_s, device_id=dev(target),
                device_id_type=pl.DeviceIdType.MESH,
            )

        @pl.when(away)
        def _():
            remote().start()

        @pl.when(own)
        def _():
            pltpu.make_async_copy(src, dst, recv_s).start()

        def done():
            @pl.when(away)
            def _():
                remote().wait_send()

        return done

    sent = []
    slot = lax.rem(c, per_part)
    part = c // per_part
    last_col = slot == per_part - 1
    first_col = (slot == 0) & (part > 0)
    quick = width - 128
    yes = r >= 0
    plan = []
    for k in range(local_rows):
        full = yes
        if k == local_rows - 1:
            full = full & (r == nr - 1)
            plan.append((k + 1, 0, WIN - 16, r < nr - 1, k))
        if k == 0:
            full = full & (r == 0)
            plan.append((k + 1, 16, WIN, r > 0, k))
        plan.append((k + 1, 0, WIN, full, k))
    plan.append((0, WIN - 16, WIN, r > 0, -1))
    plan.append((local_rows + 1, 0, 16, r < nr - 1, local_rows))
    for n, (block, lo, hi, cond, k) in enumerate(plan):
        target = (r * local_rows + k) * parts + part
        sent.append(
            push(
                cond, x_ref.at[block, pl.ds(lo, hi - lo)], recv.at[slot, pl.ds(lo, hi - lo)],
                x_send.at[n], x_recv.at[slot], target,
            )
        )
        nxt = target + 1
        sent.append(
            push(
                cond & last_col & (nxt < ndev),
                x_ref.at[block, pl.ds(lo, hi - lo), pl.ds(quick, 128)],
                recv_prev.at[pl.ds(lo, hi - lo)],
                x_prev_send.at[n], prev_recv, nxt,
            )
        )
        if parts > 1:
            sent.append(
                push(
                    cond & first_col,
                    x_ref.at[block, pl.ds(lo, hi - lo), pl.ds(0, 128)],
                    recv_next.at[pl.ds(lo, hi - lo)],
                    x_next_send.at[n], next_recv, target - 1,
                )
            )

    trans[pl.ds(0, OWN_AT)] = jnp.zeros((OWN_AT, 128), F32)
    trans[pl.ds(OWN_AT + per_part * width, 16)] = jnp.zeros((16, 128), F32)
    pad_rows = jnp.zeros((128 - WIN, 128), F32)

    def turn(block):
        return jnp.concatenate([block.astype(F32), pad_rows], 0).T

    @pl.when(me > 0)
    def _():
        pltpu.make_async_copy(recv_prev, recv_prev, prev_recv).wait()
        trans[pl.ds(16 + 128, 128)] = turn(recv_prev[...])

    for s in range(per_part):
        pltpu.make_async_copy(recv.at[s], recv.at[s], x_recv.at[s]).wait()
        for t in range(width // 128):
            trans[pl.ds(OWN_AT + s * width + t * 128, 128)] = turn(
                recv[s, :, pl.ds(t * 128, 128)]
            )

    if parts > 1:
        place = lax.rem(me, parts)

        @pl.when(place > 0)
        def _():
            trans[pl.ds(OWN_AT - 16, 4)] = trans[pl.ds(OWN_AT, 4)]
            trans[pl.ds(OWN_AT - 4, 4)] = trans[pl.ds(OWN_AT - 20, 4)]

        @pl.when(place < parts - 1)
        def _():
            pltpu.make_async_copy(recv_next, recv_next, next_recv).wait()
            trans[pl.ds(OWN_AT + per_part * width, 16)] = turn(recv_next[...])[0:16]

    for kx in range(KERNEL):
        lanes = pl.ds(kx * 128, 128)
        patches[pl.ds(0, LEAD), lanes] = trans[pl.ds(12 + kx, LEAD, stride=PATCH), :].astype(BF16)
        patches[pl.ds(LEAD, SPAN), lanes] = trans[
            pl.ds(OWN_AT - 4 + kx, SPAN, stride=PATCH), :
        ].astype(BF16)

    loads[0].wait()
    for n in range(d_model // 256):
        cs = pl.ds(n * 256, 256)
        acc = jnp.dot(patches[...], wp[:, cs], preferred_element_type=F32)
        emb[:, cs] = (acc + small_ref[pl.ds(7, 1), cs]).astype(BF16)
    resid = emb[...].astype(F32)
    mean_sq = jnp.mean(resid * resid, axis=-1, keepdims=True)
    normed[...] = (
        resid * lax.rsqrt(mean_sq + 1e-05) * small_ref[pl.ds(7, 1), pl.ds(d_model, d_model)]
    ).astype(BF16)

    own = pl.ds(LEAD, SPAN)
    step_raw = jnp.dot(normed[own], step_ref[...], preferred_element_type=F32)
    sx = step_raw + small_ref[pl.ds(8, 1), pl.ds(0, 128)]
    step = jax.nn.softplus(sx)
    log_decay = -step * jnp.exp(small_ref[pl.ds(8, 1), pl.ds(128, 128)])
    rows_i = lax.broadcasted_iota(jnp.int32, (SPAN, SPAN), 0)
    cols_i = lax.broadcasted_iota(jnp.int32, (SPAN, SPAN), 1)
    causal = rows_i >= cols_i
    cum = jnp.dot(causal.astype(F32), log_decay, precision=HI, preferred_element_type=F32)
    cum_last = cum[SPAN - 1 : SPAN, :]
    to_end = jnp.exp(cum_last - cum) * step
    logs[me] = jnp.broadcast_to(cum_last, (8, 128))
    for hop in range(1, ndev):
        target = lax.rem(me + hop, ndev)
        sent.append(
            push(
                yes, logs.at[me], logs.at[me], l_send.at[hop], l_recv.at[hop], target
            )
        )

    loads[1].wait()
    total = mixw.shape[1]
    tiles = [(lo, min(256, total - lo)) for lo in range(0, total, 256)]
    has_prev = jnp.where(me > 0, 1.0, 0.0).astype(F32)
    for lo, size in tiles[::-1]:
        cs = pl.ds(lo, size)
        proj = jnp.dot(normed[...], mixw[:, cs], preferred_element_type=F32)
        raw[:, pl.ds(0, size)] = proj.astype(BF16).astype(F32)
        raw[pl.ds(0, LEAD), pl.ds(0, size)] = raw[pl.ds(0, LEAD), pl.ds(0, size)] * has_prev
        total_sum = small_ref[pl.ds(4, 1), cs]
        for k in range(4):
            total_sum = total_sum + small_ref[pl.ds(k, 1), cs] * raw[
                pl.ds(LEAD - 3 + k, SPAN), pl.ds(0, size)
            ]
        mixed[:, cs] = jax.nn.silu(total_sum).astype(BF16)

    bc = mixed[:, pl.ds(E, 2 * NSTATE)]
    b_mat = bc[:, :NSTATE]
    c_mat = bc[:, NSTATE:]
    low_half = lax.broadcasted_iota(jnp.int32, (SPAN, 128), 1) < HDIM

    def spread(values, p):
        return jnp.where(
            low_half,
            jnp.broadcast_to(values[:, 2 * p : 2 * p + 1], (SPAN, 128)),
            jnp.broadcast_to(values[:, 2 * p + 1 : 2 * p + 2], (SPAN, 128)),
        )

    pairs = HEADS // 2
    for p in range(pairs):
        ps = pl.ds(p * 128, 128)
        xw[:, ps] = (mixed[:, ps].astype(F32) * spread(to_end, p)).astype(BF16)
    quart = E // 4
    for q in range(4):
        fresh = lax.dot_general(
            b_mat, xw[:, pl.ds(q * quart, quart)], (((0,), (0,)), ((), ())),
            preferred_element_type=F32,
        )
        squart[q] = fresh.astype(BF16)
    first = g * 4
    for hop in range(1, 4):
        other = lax.rem(e + hop, 4)
        sent.append(
            push(
                yes, squart.at[other], squart_in.at[hop - 1], q_send.at[hop], q_recv.at[hop],
                first + other,
            )
        )

    loads[2].wait()
    for n in range(E // 256):
        cs = pl.ds(n * 256, 256)
        gate[:, cs] = jnp.dot(normed[own], gatew[:, cs], preferred_element_type=F32).astype(BF16)
    scores = lax.dot_general(
        c_mat, b_mat, (((1,), (1,)), ((), ())), preferred_element_type=F32
    )
    cum_t = cum.T
    step_t = step.T

    def inside(p):
        ps = pl.ds(p * 128, 128)
        x = mixed[:, ps]
        ys = []
        for h in (2 * p, 2 * p + 1):
            gap = cum[:, h : h + 1] - cum_t[h : h + 1, :]
            decay = jnp.exp(jnp.where(causal, gap, -1e30))
            w = (scores * decay * step_t[h : h + 1, :]).astype(BF16)
            ys.append(jnp.dot(w, x, preferred_element_type=F32))
        yacc[:, ps] = jnp.where(low_half, ys[0], ys[1]) + small_ref[pl.ds(6, 1), ps] * x.astype(F32)

    for p in range(0, 4):
        inside(p)

    for hop in range(1, ndev):
        source = lax.rem(me - hop + ndev, ndev)
        pltpu.make_async_copy(logs.at[source], logs.at[source], l_recv.at[hop]).wait()
    lanes_q = lax.broadcasted_iota(jnp.int32, (128, quart), 1) + e * quart
    pick = (lanes_q // HDIM == lax.broadcasted_iota(jnp.int32, (128, quart), 0)).astype(F32)

    def expand(tile):
        return jnp.exp(jnp.dot(tile, pick, precision=HI, preferred_element_type=F32))[0:1]

    for hop in range(1, 4):
        pltpu.make_async_copy(
            squart_in.at[hop - 1], squart_in.at[hop - 1], q_recv.at[hop]
        ).wait()
    prefix = [jnp.zeros((NSTATE, quart), F32)]
    befores = [jnp.zeros((8, 128), F32)]
    for n in range(4):
        hop = lax.rem(e - n + 4, 4)
        arrived = squart_in[jnp.maximum(hop - 1, 0)].astype(F32)
        state = jnp.where(hop == 0, squart[e].astype(F32), arrived)
        tile = logs[first + n]
        prefix.append(expand(tile) * prefix[-1] + state)
        befores.append(befores[-1] + tile)
    tot_out[...] = prefix[4].astype(BF16)
    for later in range(1, ngroup):
        sent.append(
            push(
                g < later, tot_out, tot_in.at[g], t_send.at[later], t_recv.at[g], later * 4 + e
            )
        )

    for p in range(4, pairs):
        inside(p)

    inc_acc[...] = jnp.zeros_like(inc_acc)
    for k in range(ngroup - 1):

        @pl.when(k < g)
        def _():
            pltpu.make_async_copy(tot_in.at[k], tot_in.at[k], t_recv.at[k]).wait()
            tile = logs[4 * k] + logs[4 * k + 1] + logs[4 * k + 2] + logs[4 * k + 3]
            inc_acc[...] = expand(tile) * inc_acc[...] + tot_in[k].astype(F32)

    for n in range(4):
        inc_out[n] = (expand(befores[n]) * inc_acc[...] + prefix[n]).astype(BF16)
    for hop in range(1, 4):
        other = lax.rem(e + hop, 4)
        sent.append(
            push(
                yes, inc_out.at[other], inc_in.at[hop - 1], i_send.at[hop], i_recv.at[hop],
                first + other,
            )
        )
    for hop in range(1, 4):
        pltpu.make_async_copy(inc_in.at[hop - 1], inc_in.at[hop - 1], i_recv.at[hop]).wait()

    grown = jnp.exp(cum)
    sq = jnp.zeros((SPAN, 128), F32)
    for q in range(4):
        hop = lax.rem(e - q + 4, 4)
        incoming = jnp.where(hop == 0, inc_out[e], inc_in[jnp.maximum(hop - 1, 0)])
        ystate = jnp.dot(c_mat, incoming, preferred_element_type=F32)
        for n in range(quart // 128):
            p = q * (quart // 128) + n
            ps = pl.ds(p * 128, 128)
            y = yacc[:, ps] + ystate[:, n * 128 : n * 128 + 128] * spread(grown, p)
            y = y * jax.nn.silu(gate[:, ps].astype(F32))
            yacc[:, ps] = y
            sq = sq + y * y
    scale = lax.rsqrt(jnp.sum(sq, axis=-1, keepdims=True) / E + 1e-05)
    for p in range(pairs):
        ps = pl.ds(p * 128, 128)
        xw[:, ps] = (yacc[:, ps] * scale * small_ref[pl.ds(5, 1), ps]).astype(BF16)
    loads[3].wait()
    for n in range(d_model // 256):
        cs = pl.ds(n * 256, 256)
        acc = jnp.dot(xw[...], outw[:, cs], preferred_element_type=F32)
        o_ref[:, cs] = (acc + emb[own, cs].astype(F32)).astype(BF16)
    for done in sent:
        done()


def body(
    pixels, patch_weight, patch_bias, norm_gain, gate_weight, mix_weight, step_weight, step_bias,
    log_rate, conv_weight, conv_bias, skip_gain, out_gain, out_weight,
):
    cols = lax.axis_size("cols")
    nr = lax.axis_size("rows")
    chan, height, width = pixels.shape
    local_rows = height // PATCH
    ndev = cols * nr
    parts = ndev // (local_rows * nr)
    per_part = cols // parts
    ngroup = ndev // 4
    quart = E // 4
    d_model = patch_weight.shape[3]
    margin = (KERNEL - PATCH) // 2
    padded = jnp.pad(pixels, ((0, 0), (PATCH, PATCH), (0, 0))).reshape(
        chan, local_rows + 2, PATCH, width
    )
    padded = padded.transpose(1, 0, 2, 3)
    edge = jnp.zeros((1, chan, margin, width), BF16)
    top = jnp.concatenate([edge, padded[:-1, :, PATCH - margin :]], 0)
    bottom = jnp.concatenate([padded[1:, :, :margin], edge], 0)

    def rows16(a):
        a = a.reshape(a.shape[0], chan * margin, a.shape[3])
        return jnp.pad(a, ((0, 0), (0, 16 - chan * margin), (0, 0)))

    windows = jnp.concatenate(
        [rows16(top), padded.reshape(local_rows + 2, chan * PATCH, width), rows16(bottom)], 1
    )
    pw = patch_weight.transpose(1, 2, 0, 3)
    mid = KERNEL - margin
    wp = jnp.concatenate(
        [
            rows16(pw[:, :, :margin]),
            pw[:, :, margin:mid].reshape(KERNEL, chan * PATCH, d_model),
            rows16(pw[:, :, mid:]),
            jnp.zeros((KERNEL, 128 - WIN, d_model), BF16),
        ],
        1,
    ).reshape(KERNEL * 128, d_model)
    total = mix_weight.shape[1]

    def row(*vectors):
        line = jnp.concatenate(vectors)
        return jnp.pad(line, (0, total - line.shape[0]))[None]

    room = jnp.zeros((128 - HEADS,), F32)
    small = jnp.concatenate(
        [
            conv_weight,
            row(conv_bias),
            row(out_gain),
            row(jnp.repeat(skip_gain, HDIM)),
            row(patch_bias, norm_gain),
            row(step_bias, room, log_rate, room),
            jnp.zeros((7, total), F32),
        ],
        0,
    )
    step_w = jnp.pad(step_weight, ((0, 0), (0, 128 - HEADS)))
    hbm = pl.BlockSpec(memory_space=pl.ANY)
    vmem = pl.BlockSpec(memory_space=pltpu.VMEM)
    dma = pltpu.SemaphoreType.DMA
    tok = SPAN + LEAD
    return pl.pallas_call(
        functools.partial(layer_kernel, (cols, nr, local_rows, width)),
        out_shape=jax.ShapeDtypeStruct((SPAN, d_model), BF16),
        in_specs=[vmem, hbm, hbm, hbm, hbm, vmem, vmem],
        out_specs=vmem,
        scratch_shapes=[
            pltpu.VMEM(wp.shape, BF16),
            pltpu.VMEM(mix_weight.shape, BF16),
            pltpu.VMEM(gate_weight.shape, BF16),
            pltpu.VMEM(out_weight.shape, BF16),
            dma((4,)),
            pltpu.VMEM((per_part, WIN, width), BF16),
            pltpu.VMEM((WIN, 128), BF16),
            pltpu.VMEM((WIN, 128), BF16),
            pltpu.VMEM((OWN_AT + per_part * width + 16, 128), F32),
            pltpu.VMEM((tok, KERNEL * 128), BF16),
            pltpu.VMEM((tok, d_model), BF16),
            pltpu.VMEM((tok, d_model), BF16),
            pltpu.VMEM((tok, 256), F32),
            pltpu.VMEM((SPAN, total), BF16),
            pltpu.VMEM((SPAN, E), BF16),
            pltpu.VMEM((SPAN, E), F32),
            pltpu.VMEM((SPAN, E), BF16),
            pltpu.VMEM((4, NSTATE, quart), BF16),
            pltpu.VMEM((3, NSTATE, quart), BF16),
            pltpu.VMEM((ndev, 8, 128), F32),
            pltpu.VMEM((NSTATE, quart), BF16),
            pltpu.VMEM((ngroup, NSTATE, quart), BF16),
            pltpu.VMEM((4, NSTATE, quart), BF16),
            pltpu.VMEM((3, NSTATE, quart), BF16),
            pltpu.VMEM((NSTATE, quart), F32),
            dma((local_rows + 4,)),
            dma((local_rows + 4,)),
            dma((local_rows + 4,)),
            dma((per_part,)),
            dma,
            dma,
            dma((4,)),
            dma((4,)),
            dma((ndev,)),
            dma((ndev,)),
            dma((ngroup,)),
            dma((ngroup,)),
            dma((4,)),
            dma((4,)),
        ],
        compiler_params=pltpu.CompilerParams(
            collective_id=0, has_side_effects=True, vmem_limit_bytes=56 * 1024 * 1024
        ),
    )(windows, wp, mix_weight, gate_weight, out_weight, step_w, small)


def solution(mesh):
    placed = (
        P(None, "rows", ("slides", "cols")),
        P(),
        P(),
        P(),
        P(),
        P(),
        P(),
        P(),
        P(),
        P(),
        P(),
        P(),
        P(),
        P(),
    )
    return jax.shard_map(
        body,
        mesh=mesh,
        in_specs=placed,
        out_specs=P(("slides", "cols", "rows"), None),
        check_vma=False,
    )
```

time: 243 us -> 58.4 us (0.24)
  matrix products: 60 us -> 0 us
  Pallas kernels: 0 us -> 46.2 us
  local copies, waits for them, and re-layouts: 49.2 us -> 7.22 us
  waiting for transfers between devices: 40.2 us -> 0 us
  blocking collectives: 35 us -> 0 us
  other arithmetic: 24.8 us -> 4.01 us
  starting transfers between devices: 16.8 us -> 0 us
  between operations: 14.6 us -> 0.27 us
    pallas_call x0 -> x1, Pallas kernels: none -> 46.2 us  [body(): pl.pallas_call(functools.partial(layer_kernel, (cols, nr, local_rows, wid...]
    conv_general_dilated x1 -> x0, matrix products: 40.8 us -> none  [body(): lax.conv_general_dilated(padded[None], patch_weight, (PATCH, PATCH), 'VAL...]
    all_gather x1 -> x0, waiting for transfers between devices: 24.2 us -> none  [carried_in(): lax.all_gather(a.astype(kind), axis)]
    dot_general x8 -> x0, matrix products: 19.2 us -> none  [the longest x1 4.58 us: body(): jnp.einsum('chts,cshp->cthp', weights, head_in, preferred_element_type=jn...]
    unnamed x1 -> x0, blocking collectives: 17.7 us -> none
    conv_general_dilated x6 -> x0, local copies, waits for them, and re-layouts: 17.3 us -> none  [body(): lax.conv_general_dilated(padded[None], patch_weight, (PATCH, PATCH), 'VAL...]
    all_to_all x1 -> x0, blocking collectives: 17.3 us -> none  [body(): lax.all_to_all(outgoing, ('cols', 'rows'), split_axis=1, concat_axis=1, t...]
    ppermute x7 -> x0, starting transfers between devices: 10.8 us -> none  [the longest x2 5.84 us: extended(): lax.ppermute(lax.slice_in_dim(block, 0, width, axis=dim), axis, backward)]
  transfers between devices with their start and end apart: 9 -> 0, of which waited for: 8 -> 0; matrix products, arithmetic and copies ran while one was open for 8% -> 0% of each run, Pallas kernels for 0% -> 0%
where the time goes in v1:
time: 58.4 us; the launch traced here: 57.7 us
  Pallas kernels  46.2 us (79%)
  local copies, waits for them, and re-layouts  7.22 us (12%)
  other arithmetic  4.01 us (7%)
    pallas_call x1, Pallas kernels, body(): pl.pallas_call(functools.partial(layer_kernel, (cols, nr, local_rows, wid...  46.2 us
    unnamed x24, local copies, waits for them, and re-layouts  3.98 us
    concatenate x1, other arithmetic, body(): jnp.concatenate([rows16(pw[:, :, :margin]), pw[:, :, margin:mid].reshape(...  2.92 us
    concatenate x1, local copies, waits for them, and re-layouts, body(): jnp.concatenate([conv_weight, row(conv_bias), row(out_gain), row(jnp.repe...  1.31 us

profile of v1, /device:TPU:28, one launch (start us, length us, event | category | flops | bytes accessed | tf_op | source)
XLA Modules:
  0.0 57.7 jit_solution(15038066499320610226)
XLA Ops:
  0.0 1.9 %copy.27 = bf16[24,24,3,768]{3,1,0,2:T(8,128)(2,1)S(1)} copy(bf16[24,24,3,768]{3,1,2,0:T(8,128)(2,1)} %param.15) | data formatting | bytes 5308416 | tf_op args[1]
  1.9 0.1 fusion.10
  2.0 0.1 copy.20
  2.1 0.1 copy.23
  2.2 0.1 slice.23
  2.3 0.3 copy.19
  2.6 0.0 copy-start
  2.7 0.1 pad.57.clone
  2.7 2.9 %fusion.4 = bf16[24,128,768]{2,1,0:T(8,128)(2,1)} fusion(bf16[24,12,768]{2,1,0:T(8,128)(2,1)S(1)} %copy.20, bf16[24,12,768]{2,1,0:T(8,128)(2,1)S(1)} %copy.23, bf16[24,48,768]{2,1,0:T(8,128)(2,1)S(1)} %bitcast.15, bf16[128]{0:T(256)(128)(2,1)S(1)} %pad.57.clone), kind=kLoop, calls=%fused_computation.7 | loop fusion | flops 33030144 | bytes 7373056 | tf_op jit(solution)/shard_map/concatenate | solution.py:395
  5.7 0.0 copy-start.5
  5.7 0.0 copy-start.6
  5.7 0.0 copy-start.4
  5.7 0.0 copy-start.2
  5.7 0.0 copy-done
  5.8 0.1 fusion.12
  6.1 1.0 %fusion.8.x_ref = bf16[10,80,512]{2,1,0:T(8,128)(2,1)} fusion(bf16[10,12,512]{2,1,0:T(8,128)(2,1)S(1)} %reshape.30, bf16[10,12,512]{2,1,0:T(8,128)(2,1)S(1)} %reshape.28, bf16[10,48,512]{2,1,0:T(8,128)(2,1)S(1)} %bitcast.17), kind=kLoop, calls=%fused_computation.14 | loop fusion | flops 4096000 | bytes 1556480 | tf_op jit(solution)/shard_map/concatenate | solution.py:390
  7.1 0.0 copy-done.1
  7.1 0.2 copy.22
  7.3 0.7 %pad.43.step_ref = bf16[768,128]{1,0:T(8,128)(2,1)} pad(bf16[768,24]{1,0:T(8,128)(2,1)S(1)} %copy.22, bf16[]{:T(256)} %constant.2.clone.1), padding=0_0x0_104 | pad | bytes 233474 | tf_op jit(solution)/shard_map/jit(_pad)/pad | solution.py:423
  8.0 0.0 copy-done.7
  8.0 0.1 broadcast_in_dim.31
  8.1 0.1 reshape.35
  8.2 0.0 copy-done.8
  8.2 0.0 copy-done.9
  8.2 0.1 select_maximum_fusion
  8.3 0.0 copy-done.3
  8.3 0.0 copy-done.5
  8.3 0.0 copy-done.6
  8.4 0.0 copy-done.2
  8.4 1.3 %concatenate.27.small_ref = f32[16,1664]{1,0:T(8,128)} concatenate(f32[4,1664]{1,0:T(4,128)S(1)} %copy-done.2, f32[1,1664]{1,0:T(1,128)S(1)} %broadcast_in_dim.29, f32[1,1664]{1,0:T(1,128)S(1)} %broadcast_in_dim.30, f32[1,1664]{1,0:T(1,128)S(1)} %broadcast_in_dim.32, f32[1,1664]{1,0:T(1,128)S(1)} %broadcast_in_dim.33, f32[1,1664]{1,0:T(1,128)S(1)} %broadcast_in_dim.35, ...), dimensions={0} | concatenate | bytes 212992 | tf_op jit(solution)/shard_map/concatenate | solution.py:411
  9.7 46.2 %shard_map.136 = bf16[256,768]{1,0:T(8,128)(2,1)} custom-call(bf16[10,80,512]{2,1,0:T(8,128)(2,1)} %fusion.8.x_ref, bf16[3072,768]{1,0:T(8,128)(2,1)} %bitcast.12, bf16[768,1664]{1,0:T(8,128)(2,1)} %mix_hbm.1, bf16[768,1536]{1,0:T(8,128)(2,1)} %gate_hbm.1, bf16[1536,768]{1,0:T(8,128)(2,1)} %out_hbm.1, bf16[768,128]{1,0:T(8,128)(2,1)} %pad.43.step_ref, ...), custom_call_target="tpu_custom_call" | custom-call | tf_op jit(solution)/shard_map/pallas_call | solution.py:428
  55.9 1.8 %copy.30 = bf16[256,768]{1,0:T(8,128)(2,1)} copy(bf16[256,768]{1,0:T(8,128)(2,1)} %shard_map.136) | data formatting | bytes 786432
  (23 shorter events, 0.3 us)
Async XLA Ops:
  2.6 3.1 %copy-start = (bf16[3,128,512]{2,1,0:T(8,128)(2,1)S(1)}, bf16[3,128,512]{2,1,0:T(8,128)(2,1)}, u32[]{:S(2)}) copy-start(bf16[3,128,512]{2,1,0:T(8,128)(2,1)} %param.14) | copy-start | bytes 1179652
  2.7 4.4 %copy-start.1 = (bf16[768,24]{0,1:T(8,128)(2,1)S(1)}, bf16[768,24]{0,1:T(8,128)(2,1)}, u32[]{:S(2)}) copy-start(bf16[768,24]{0,1:T(8,128)(2,1)} %param.20) | copy-start | bytes 110596
  5.7 2.4 %copy-start.7 = (f32[24]{0:T(128)S(1)}, f32[24]{0:T(128)}, u32[]{:S(2)}) copy-start(f32[24]{0:T(128)} %param.25) | copy-start | bytes 292
  5.7 2.5 %copy-start.8 = (f32[24]{0:T(128)S(1)}, f32[24]{0:T(128)}, u32[]{:S(2)}) copy-start(f32[24]{0:T(128)} %param.22) | copy-start | bytes 292
  5.7 2.5 %copy-start.9 = (f32[24]{0:T(128)S(1)}, f32[24]{0:T(128)}, u32[]{:S(2)}) copy-start(f32[24]{0:T(128)} %param.21) | copy-start | bytes 292
  5.7 2.6 %copy-start.3 = (f32[1536]{0:T(1024)S(1)}, f32[1536]{0:T(1024)}, u32[]{:S(2)}) copy-start(f32[1536]{0:T(1024)} %param.26) | copy-start | bytes 18436
  5.7 2.7 %copy-start.5 = (f32[768]{0:T(1024)S(1)}, f32[768]{0:T(1024)}, u32[]{:S(2)}) copy-start(f32[768]{0:T(1024)} %param.17) | copy-start | bytes 9220
  5.7 2.7 %copy-start.6 = (f32[768]{0:T(1024)S(1)}, f32[768]{0:T(1024)}, u32[]{:S(2)}) copy-start(f32[768]{0:T(1024)} %param.16) | copy-start | bytes 9220
  5.7 2.7 %copy-start.4 = (f32[1664]{0:T(1024)S(1)}, f32[1664]{0:T(1024)}, u32[]{:S(2)}) copy-start(f32[1664]{0:T(1024)} %param.24) | copy-start | bytes 19972
  5.7 2.7 %copy-start.2 = (f32[4,1664]{1,0:T(4,128)S(1)}, f32[4,1664]{1,0:T(4,128)}, u32[]{:S(2)}) copy-start(f32[4,1664]{1,0:T(4,128)} %param.23) | copy-start | bytes 79876

commit v2 on v1

--- a/solution.py
+++ b/solution.py
@@ -27,7 +27,7 @@
 
 def layer_kernel(
     dims, x_ref, wp_hbm, mix_hbm, gate_hbm, out_hbm, step_ref, small_ref, o_ref,
-    wp, mixw, gatew, outw, w_sem,
+    wp_raw, wide, wp, mixw, gatew, outw, w_sem,
     recv, recv_prev, recv_next, trans, patches, emb, normed, raw, mixed, gate, yacc, xw,
     squart, squart_in, logs, tot_out, tot_in, inc_out, inc_in, inc_acc,
     x_send, x_prev_send, x_next_send, x_recv, prev_recv, next_recv,
@@ -51,7 +51,7 @@
     loads = [
         pltpu.make_async_copy(s, t, w_sem.at[n])
         for n, (s, t) in enumerate(
-            ((wp_hbm, wp), (mix_hbm, mixw), (gate_hbm, gatew), (out_hbm, outw))
+            ((wp_hbm, wp_raw), (mix_hbm, mixw), (gate_hbm, gatew), (out_hbm, outw))
         )
     ]
     for load in loads:
@@ -91,54 +91,85 @@
         return done
 
     sent = []
+    yes = r >= 0
     slot = lax.rem(c, per_part)
     part = c // per_part
     last_col = slot == per_part - 1
     first_col = (slot == 0) & (part > 0)
-    quick = width - 128
-    yes = r >= 0
-    plan = []
-    for k in range(local_rows):
-        full = yes
-        if k == local_rows - 1:
-            full = full & (r == nr - 1)
-            plan.append((k + 1, 0, WIN - 16, r < nr - 1, k))
-        if k == 0:
-            full = full & (r == 0)
-            plan.append((k + 1, 16, WIN, r > 0, k))
-        plan.append((k + 1, 0, WIN, full, k))
-    plan.append((0, WIN - 16, WIN, r > 0, -1))
-    plan.append((local_rows + 1, 0, 16, r < nr - 1, local_rows))
-    for n, (block, lo, hi, cond, k) in enumerate(plan):
-        target = (r * local_rows + k) * parts + part
+    band = CHAN * PATCH
+
+    def send_rows(n, cond, start, lo, size, target):
+        src = x_ref.at[pl.ds(start, size)]
         sent.append(
             push(
-                cond, x_ref.at[block, pl.ds(lo, hi - lo)], recv.at[slot, pl.ds(lo, hi - lo)],
-                x_send.at[n], x_recv.at[slot], target,
-            )
-        )
-        nxt = target + 1
+                cond, src, recv.at[slot, pl.ds(lo, size)], x_send.at[n], x_recv.at[slot], target
+            )
+        )
+        src = x_ref.at[pl.ds(start, size), pl.ds(width - 128, 128)]
         sent.append(
             push(
-                cond & last_col & (nxt < ndev),
-                x_ref.at[block, pl.ds(lo, hi - lo), pl.ds(quick, 128)],
-                recv_prev.at[pl.ds(lo, hi - lo)],
-                x_prev_send.at[n], prev_recv, nxt,
+                cond & last_col & (target + 1 < ndev), src, recv_prev.at[pl.ds(lo, size)],
+                x_prev_send.at[n], prev_recv, target + 1,
             )
         )
         if parts > 1:
+            src = x_ref.at[pl.ds(start, size), pl.ds(0, 128)]
             sent.append(
                 push(
-                    cond & first_col,
-                    x_ref.at[block, pl.ds(lo, hi - lo), pl.ds(0, 128)],
-                    recv_next.at[pl.ds(lo, hi - lo)],
+                    cond & first_col, src, recv_next.at[pl.ds(lo, size)],
                     x_next_send.at[n], next_recv, target - 1,
                 )
             )
+
+    def holder(k):
+        return (r * local_rows + k) * parts + part
+
+    edge_low = r > 0
+    edge_high = r < nr - 1
+    for n in range(local_rows):
+        k = lax.rem(n + c, local_rows)
+        start = pl.multiple_of(k * band, 16)
+        cut_low = edge_low & (k == 0)
+        cut_high = edge_high & (k == local_rows - 1)
+        send_rows(n, jnp.logical_not(cut_low | cut_high), start, 0, WIN, holder(k))
+    send_rows(local_rows, edge_low, 16, 16, WIN - 16, holder(0))
+    send_rows(
+        local_rows + 1, edge_high, (local_rows - 1) * band, 0, WIN - 16, holder(local_rows - 1)
+    )
+    send_rows(local_rows + 2, edge_low, 16, WIN - 16, 16, holder(0) - parts)
+    send_rows(
+        local_rows + 3, edge_high, local_rows * band, 0, 16, holder(local_rows - 1) + parts
+    )
 
     trans[pl.ds(0, OWN_AT)] = jnp.zeros((OWN_AT, 128), F32)
     trans[pl.ds(OWN_AT + per_part * width, 16)] = jnp.zeros((16, 128), F32)
     pad_rows = jnp.zeros((128 - WIN, 128), F32)
+
+    lane_tiles = d_model // 128
+    for n in range(lane_tiles):
+        wide[n, pl.ds(0, 96)] = jnp.zeros((96, 128), F32)
+        wide[n, pl.ds(96 + KERNEL * CHAN * KERNEL, 96)] = jnp.zeros((96, 128), F32)
+    loads[0].wait()
+    step_rows = CHAN * KERNEL
+
+    def widen(n, _):
+        at = pl.multiple_of(n * step_rows, 8)
+        for t in range(lane_tiles):
+            line = wp_raw[n, :, pl.ds(t * 128, 128)].astype(F32)
+            wide[t, pl.ds(pl.multiple_of(96 + at, 8), step_rows)] = line
+        return 0
+
+    lax.fori_loop(0, KERNEL, widen, 0)
+
+    def regroup(kx, _):
+        at = pl.multiple_of(kx * 128, 128)
+        for n in range(lane_tiles):
+            part_n = wide.at[n][pl.ds(kx, WIN, stride=KERNEL), :]
+            wp[pl.ds(at, WIN), pl.ds(n * 128, 128)] = part_n.astype(BF16)
+        wp[pl.ds(pl.multiple_of(at + WIN, 16), 128 - WIN)] = jnp.zeros((128 - WIN, d_model), BF16)
+        return 0
+
+    lax.fori_loop(0, KERNEL, regroup, 0)
 
     def turn(block):
         return jnp.concatenate([block.astype(F32), pad_rows], 0).T
@@ -175,7 +206,6 @@
             pl.ds(OWN_AT - 4 + kx, SPAN, stride=PATCH), :
         ].astype(BF16)
 
-    loads[0].wait()
     for n in range(d_model // 256):
         cs = pl.ds(n * 256, 256)
         acc = jnp.dot(patches[...], wp[:, cs], preferred_element_type=F32)
@@ -374,33 +404,10 @@
     ngroup = ndev // 4
     quart = E // 4
     d_model = patch_weight.shape[3]
-    margin = (KERNEL - PATCH) // 2
-    padded = jnp.pad(pixels, ((0, 0), (PATCH, PATCH), (0, 0))).reshape(
-        chan, local_rows + 2, PATCH, width
-    )
-    padded = padded.transpose(1, 0, 2, 3)
-    edge = jnp.zeros((1, chan, margin, width), BF16)
-    top = jnp.concatenate([edge, padded[:-1, :, PATCH - margin :]], 0)
-    bottom = jnp.concatenate([padded[1:, :, :margin], edge], 0)
-
-    def rows16(a):
-        a = a.reshape(a.shape[0], chan * margin, a.shape[3])
-        return jnp.pad(a, ((0, 0), (0, 16 - chan * margin), (0, 0)))
-
-    windows = jnp.concatenate(
-        [rows16(top), padded.reshape(local_rows + 2, chan * PATCH, width), rows16(bottom)], 1
-    )
-    pw = patch_weight.transpose(1, 2, 0, 3)
-    mid = KERNEL - margin
-    wp = jnp.concatenate(
-        [
-            rows16(pw[:, :, :margin]),
-            pw[:, :, margin:mid].reshape(KERNEL, chan * PATCH, d_model),
-            rows16(pw[:, :, mid:]),
-            jnp.zeros((KERNEL, 128 - WIN, d_model), BF16),
-        ],
-        1,
-    ).reshape(KERNEL * 128, d_model)
+    windows = jnp.pad(
+        pixels.transpose(1, 0, 2).reshape(height * chan, width), ((16, 16), (0, 0))
+    )
+    wp = patch_weight.transpose(0, 2, 1, 3).reshape(KERNEL, CHAN * KERNEL, d_model)
     total = mix_weight.shape[1]
 
     def row(*vectors):
@@ -432,6 +439,8 @@
         out_specs=vmem,
         scratch_shapes=[
             pltpu.VMEM(wp.shape, BF16),
+            pltpu.VMEM((d_model // 128, 96 + KERNEL * CHAN * KERNEL + 96, 128), F32),
+            pltpu.VMEM((KERNEL * 128, d_model), BF16),
             pltpu.VMEM(mix_weight.shape, BF16),
             pltpu.VMEM(gate_weight.shape, BF16),
             pltpu.VMEM(out_weight.shape, BF16),

time: 58.4 us -> 52.7 us (0.902)
  other arithmetic: 4.01 us -> 0.09 us
  Pallas kernels: 46.2 us -> 44.8 us
    concatenate x2 -> x0, other arithmetic: 3.93 us -> none  [the longest x1 2.92 us: body(): jnp.concatenate([rows16(pw[:, :, :margin]), pw[:, :, margin:mid].reshape(...]
    unnamed x24 -> x20, local copies, waits for them, and re-layouts: 3.98 us -> 1.97 us
    transpose x0 -> x1, local copies, waits for them, and re-layouts: none -> 1.41 us  [body(): pixels.transpose(1, 0, 2).reshape(height * chan, width)]
    pallas_call x1, Pallas kernels: 46.2 us -> 44.8 us  [body(): pl.pallas_call(functools.partial(layer_kernel, (cols, nr, local_rows, wid...]
    pad x1, local copies, waits for them, and re-layouts: 0.04 us -> 0.79 us  [body(): jnp.pad(pixels.transpose(1, 0, 2).reshape(height * chan, width), ((16, 16...]
    slice x4 -> x0, local copies, waits for them, and re-layouts: 0.6 us -> none  [the longest x2 0.45 us: body(): pw[:, :, margin:mid].reshape(KERNEL, chan * PATCH, d_model)]
where the time goes in v2:
time: 52.7 us; the launch traced here: 51.8 us
  Pallas kernels  44.8 us (85%)
  local copies, waits for them, and re-layouts  6.73 us (13%)
    pallas_call x1, Pallas kernels, body(): pl.pallas_call(functools.partial(layer_kernel, (cols, nr, local_rows, wid...  44.8 us
    unnamed x20, local copies, waits for them, and re-layouts  1.97 us
    transpose x1, local copies, waits for them, and re-layouts, body(): pixels.transpose(1, 0, 2).reshape(height * chan, width)  1.41 us
    concatenate x1, local copies, waits for them, and re-layouts, body(): jnp.concatenate([conv_weight, row(conv_bias), row(out_gain), row(jnp.repe...  1.31 us

profile of v2, /device:TPU:28, one launch (start us, length us, event | category | flops | bytes accessed | tf_op | source)
XLA Modules:
  0.0 51.8 jit_solution(4789444210488320362)
XLA Ops:
  0.0 0.0 copy-start
  0.0 0.0 copy-start.6
  0.0 0.0 copy-start.8
  0.0 0.0 copy-start.7
  0.0 0.0 copy-start.2
  0.0 0.0 copy-start.5
  0.0 0.0 copy-start.4
  0.0 0.0 copy-start.3
  0.1 0.0 copy-start.1
  0.1 1.4 %copy.17 = bf16[128,3,512]{2,1,0:T(4,128)(2,1)S(1)} copy(bf16[128,3,512]{2,0,1:T(8,128)(2,1)} %bitcast.5) | data formatting | bytes 786432 | tf_op jit(solution)/shard_map/transpose | solution.py:408
  1.5 0.3 reshape.9
  1.8 0.8 %pad.22.x_ref = bf16[416,512]{1,0:T(8,128)(2,1)} pad(bf16[384,512]{1,0:T(8,128)(2,1)S(1)} %reshape.9, bf16[]{:T(256)} %constant.2.clone.1), padding=16_16x0_0 | pad | bytes 819202 | tf_op jit(solution)/shard_map/jit(_pad)/pad | solution.py:407
  2.6 0.0 copy-done
  2.6 0.2 copy.18
  2.8 0.7 %pad.23.step_ref = bf16[768,128]{1,0:T(8,128)(2,1)} pad(bf16[768,24]{1,0:T(8,128)(2,1)S(1)} %copy.18, bf16[]{:T(256)} %constant.2.clone.1), padding=0_0x0_104 | pad | bytes 233474 | tf_op jit(solution)/shard_map/jit(_pad)/pad | solution.py:430
  3.5 0.0 copy-done.6
  3.5 0.1 broadcast_in_dim.26
  3.6 0.1 reshape.11
  3.7 0.0 copy-done.8
  3.7 0.0 copy-done.7
  3.7 0.1 select_maximum_fusion
  3.8 0.0 copy-done.2
  3.8 0.0 copy-done.5
  3.8 0.0 copy-done.4
  3.9 0.0 copy-done.3
  3.9 0.0 copy-done.1
  3.9 1.3 %concatenate.11.small_ref = f32[16,1664]{1,0:T(8,128)} concatenate(f32[4,1664]{1,0:T(4,128)S(1)} %copy-done.1, f32[1,1664]{1,0:T(1,128)S(1)} %broadcast_in_dim.24, f32[1,1664]{1,0:T(1,128)S(1)} %broadcast_in_dim.25, f32[1,1664]{1,0:T(1,128)S(1)} %broadcast_in_dim.27, f32[1,1664]{1,0:T(1,128)S(1)} %broadcast_in_dim.28, f32[1,1664]{1,0:T(1,128)S(1)} %broadcast_in_dim.30, ...), dimensions={0} | concatenate | bytes 212992 | tf_op jit(solution)/shard_map/concatenate | solution.py:418
  5.2 44.8 %shard_map.136 = bf16[256,768]{1,0:T(8,128)(2,1)} custom-call(bf16[416,512]{1,0:T(8,128)(2,1)} %pad.22.x_ref, bf16[24,72,768]{2,1,0:T(8,128)(2,1)} %bitcast.4, bf16[768,1664]{1,0:T(8,128)(2,1)} %mix_hbm.1, bf16[768,1536]{1,0:T(8,128)(2,1)} %gate_hbm.1, bf16[1536,768]{1,0:T(8,128)(2,1)} %out_hbm.1, bf16[768,128]{1,0:T(8,128)(2,1)} %pad.23.step_ref, ...), custom_call_target="tpu_custom_call" | custom-call | tf_op jit(solution)/shard_map/pallas_call | solution.py:435
  50.1 1.8 %copy.20 = bf16[256,768]{1,0:T(8,128)(2,1)} copy(bf16[256,768]{1,0:T(8,128)(2,1)} %shard_map.136) | data formatting | bytes 786432
  (10 shorter events, 0.1 us)
Async XLA Ops:
  0.0 2.6 %copy-start = (bf16[768,24]{0,1:T(8,128)(2,1)S(1)}, bf16[768,24]{0,1:T(8,128)(2,1)}, u32[]{:S(2)}) copy-start(bf16[768,24]{0,1:T(8,128)(2,1)} %param.20) | copy-start | bytes 110596
  0.0 3.5 %copy-start.6 = (f32[24]{0:T(128)S(1)}, f32[24]{0:T(128)}, u32[]{:S(2)}) copy-start(f32[24]{0:T(128)} %param.25) | copy-start | bytes 292
  0.0 3.7 %copy-start.8 = (f32[24]{0:T(128)S(1)}, f32[24]{0:T(128)}, u32[]{:S(2)}) copy-start(f32[24]{0:T(128)} %param.21) | copy-start | bytes 292
  0.0 3.7 %copy-start.7 = (f32[24]{0:T(128)S(1)}, f32[24]{0:T(128)}, u32[]{:S(2)}) copy-start(f32[24]{0:T(128)} %param.22) | copy-start | bytes 292
  0.0 3.8 %copy-start.2 = (f32[1536]{0:T(1024)S(1)}, f32[1536]{0:T(1024)}, u32[]{:S(2)}) copy-start(f32[1536]{0:T(1024)} %param.26) | copy-start | bytes 18436
  0.0 3.8 %copy-start.5 = (f32[768]{0:T(1024)S(1)}, f32[768]{0:T(1024)}, u32[]{:S(2)}) copy-start(f32[768]{0:T(1024)} %param.16) | copy-start | bytes 9220
  0.0 3.8 %copy-start.4 = (f32[768]{0:T(1024)S(1)}, f32[768]{0:T(1024)}, u32[]{:S(2)}) copy-start(f32[768]{0:T(1024)} %param.17) | copy-start | bytes 9220
  0.0 3.8 %copy-start.3 = (f32[1664]{0:T(1024)S(1)}, f32[1664]{0:T(1024)}, u32[]{:S(2)}) copy-start(f32[1664]{0:T(1024)} %param.24) | copy-start | bytes 19972
  0.1 3.8 %copy-start.1 = (f32[4,1664]{1,0:T(4,128)S(1)}, f32[4,1664]{1,0:T(4,128)}, u32[]{:S(2)}) copy-start(f32[4,1664]{1,0:T(4,128)} %param.23) | copy-start | bytes 79876

commit v3 on v2

--- a/solution.py
+++ b/solution.py
@@ -26,7 +26,8 @@
 
 
 def layer_kernel(
-    dims, x_ref, wp_hbm, mix_hbm, gate_hbm, out_hbm, step_ref, small_ref, o_ref,
+    dims, x_ref, wp_hbm, mix_hbm, gate_hbm, out_hbm, step_ref, tap_ref, conv_b_ref,
+    gain_ref, skip_ref, patch_b_ref, norm_g_ref, bias_ref, rate_ref, o_ref,
     wp_raw, wide, wp, mixw, gatew, outw, w_sem,
     recv, recv_prev, recv_next, trans, patches, emb, normed, raw, mixed, gate, yacc, xw,
     squart, squart_in, logs, tot_out, tot_in, inc_out, inc_in, inc_acc,
@@ -209,25 +210,33 @@
     for n in range(d_model // 256):
         cs = pl.ds(n * 256, 256)
         acc = jnp.dot(patches[...], wp[:, cs], preferred_element_type=F32)
-        emb[:, cs] = (acc + small_ref[pl.ds(7, 1), cs]).astype(BF16)
+        emb[:, cs] = (acc + patch_b_ref[:, cs]).astype(BF16)
     resid = emb[...].astype(F32)
     mean_sq = jnp.mean(resid * resid, axis=-1, keepdims=True)
     normed[...] = (
-        resid * lax.rsqrt(mean_sq + 1e-05) * small_ref[pl.ds(7, 1), pl.ds(d_model, d_model)]
+        resid * lax.rsqrt(mean_sq + 1e-05) * norm_g_ref[...]
     ).astype(BF16)
 
     own = pl.ds(LEAD, SPAN)
-    step_raw = jnp.dot(normed[own], step_ref[...], preferred_element_type=F32)
-    sx = step_raw + small_ref[pl.ds(8, 1), pl.ds(0, 128)]
+    step_raw = lax.dot_general(
+        normed[own], step_ref[...], (((1,), (1,)), ((), ())), preferred_element_type=F32
+    )
+    sx = step_raw + bias_ref[...]
     step = jax.nn.softplus(sx)
-    log_decay = -step * jnp.exp(small_ref[pl.ds(8, 1), pl.ds(128, 128)])
+    log_decay = -step * jnp.exp(rate_ref[...])
     rows_i = lax.broadcasted_iota(jnp.int32, (SPAN, SPAN), 0)
     cols_i = lax.broadcasted_iota(jnp.int32, (SPAN, SPAN), 1)
     causal = rows_i >= cols_i
     cum = jnp.dot(causal.astype(F32), log_decay, precision=HI, preferred_element_type=F32)
     cum_last = cum[SPAN - 1 : SPAN, :]
     to_end = jnp.exp(cum_last - cum) * step
-    logs[me] = jnp.broadcast_to(cum_last, (8, 128))
+    unit = (
+        lax.broadcasted_iota(jnp.int32, (HEADS, 128), 0)
+        == lax.broadcasted_iota(jnp.int32, (HEADS, 128), 1)
+    ).astype(F32)
+    logs[me] = jnp.dot(
+        jnp.broadcast_to(cum_last, (8, HEADS)), unit, precision=HI, preferred_element_type=F32
+    )
     for hop in range(1, ndev):
         target = lax.rem(me + hop, ndev)
         sent.append(
@@ -245,9 +254,9 @@
         proj = jnp.dot(normed[...], mixw[:, cs], preferred_element_type=F32)
         raw[:, pl.ds(0, size)] = proj.astype(BF16).astype(F32)
         raw[pl.ds(0, LEAD), pl.ds(0, size)] = raw[pl.ds(0, LEAD), pl.ds(0, size)] * has_prev
-        total_sum = small_ref[pl.ds(4, 1), cs]
+        total_sum = conv_b_ref[:, cs]
         for k in range(4):
-            total_sum = total_sum + small_ref[pl.ds(k, 1), cs] * raw[
+            total_sum = total_sum + tap_ref[pl.ds(k, 1), cs] * raw[
                 pl.ds(LEAD - 3 + k, SPAN), pl.ds(0, size)
             ]
         mixed[:, cs] = jax.nn.silu(total_sum).astype(BF16)
@@ -304,9 +313,12 @@
             decay = jnp.exp(jnp.where(causal, gap, -1e30))
             w = (scores * decay * step_t[h : h + 1, :]).astype(BF16)
             ys.append(jnp.dot(w, x, preferred_element_type=F32))
-        yacc[:, ps] = jnp.where(low_half, ys[0], ys[1]) + small_ref[pl.ds(6, 1), ps] * x.astype(F32)
-
-    for p in range(0, 4):
+        skip = jnp.where(
+            low_half, skip_ref[:, 2 * p : 2 * p + 1], skip_ref[:, 2 * p + 1 : 2 * p + 2]
+        )
+        yacc[:, ps] = jnp.where(low_half, ys[0], ys[1]) + skip * x.astype(F32)
+
+    for p in range(0, 2):
         inside(p)
 
     for hop in range(1, ndev):
@@ -339,7 +351,7 @@
             )
         )
 
-    for p in range(4, pairs):
+    for p in range(2, 8):
         inside(p)
 
     inc_acc[...] = jnp.zeros_like(inc_acc)
@@ -361,6 +373,8 @@
                 first + other,
             )
         )
+    for p in range(8, pairs):
+        inside(p)
     for hop in range(1, 4):
         pltpu.make_async_copy(inc_in.at[hop - 1], inc_in.at[hop - 1], i_recv.at[hop]).wait()
 
@@ -380,7 +394,7 @@
     scale = lax.rsqrt(jnp.sum(sq, axis=-1, keepdims=True) / E + 1e-05)
     for p in range(pairs):
         ps = pl.ds(p * 128, 128)
-        xw[:, ps] = (yacc[:, ps] * scale * small_ref[pl.ds(5, 1), ps]).astype(BF16)
+        xw[:, ps] = (yacc[:, ps] * scale * gain_ref[:, ps]).astype(BF16)
     loads[3].wait()
     for n in range(d_model // 256):
         cs = pl.ds(n * 256, 256)
@@ -410,24 +424,6 @@
     wp = patch_weight.transpose(0, 2, 1, 3).reshape(KERNEL, CHAN * KERNEL, d_model)
     total = mix_weight.shape[1]
 
-    def row(*vectors):
-        line = jnp.concatenate(vectors)
-        return jnp.pad(line, (0, total - line.shape[0]))[None]
-
-    room = jnp.zeros((128 - HEADS,), F32)
-    small = jnp.concatenate(
-        [
-            conv_weight,
-            row(conv_bias),
-            row(out_gain),
-            row(jnp.repeat(skip_gain, HDIM)),
-            row(patch_bias, norm_gain),
-            row(step_bias, room, log_rate, room),
-            jnp.zeros((7, total), F32),
-        ],
-        0,
-    )
-    step_w = jnp.pad(step_weight, ((0, 0), (0, 128 - HEADS)))
     hbm = pl.BlockSpec(memory_space=pl.ANY)
     vmem = pl.BlockSpec(memory_space=pltpu.VMEM)
     dma = pltpu.SemaphoreType.DMA
@@ -435,7 +431,7 @@
     return pl.pallas_call(
         functools.partial(layer_kernel, (cols, nr, local_rows, width)),
         out_shape=jax.ShapeDtypeStruct((SPAN, d_model), BF16),
-        in_specs=[vmem, hbm, hbm, hbm, hbm, vmem, vmem],
+        in_specs=[vmem, hbm, hbm, hbm, hbm] + [vmem] * 9,
         out_specs=vmem,
         scratch_shapes=[
             pltpu.VMEM(wp.shape, BF16),
@@ -483,7 +479,11 @@
         compiler_params=pltpu.CompilerParams(
             collective_id=0, has_side_effects=True, vmem_limit_bytes=56 * 1024 * 1024
         ),
-    )(windows, wp, mix_weight, gate_weight, out_weight, step_w, small)
+    )(
+        windows, wp, mix_weight, gate_weight, out_weight, step_weight.T, conv_weight,
+        conv_bias[None], out_gain[None], skip_gain[None], patch_bias[None], norm_gain[None],
+        step_bias[None], log_rate[None],
+    )
 
 
 def solution(mesh):

time: 52.7 us -> 52.5 us (level)
    broadcast_in_dim x8 -> x4, local copies, waits for them, and re-layouts: 0.11 us -> 2.38 us  [the longest x1 0.6 us: body(): conv_bias[None]]
    concatenate x1 -> x0, local copies, waits for them, and re-layouts: 1.31 us -> none  [body(): jnp.concatenate([conv_weight, row(conv_bias), row(out_gain), row(jnp.repe...]
    pad x3 -> x0, local copies, waits for them, and re-layouts: 0.74 us -> none  [the longest x1 0.72 us: body(): step_w = jnp.pad(step_weight, ((0, 0), (0, 128 - HEADS)))]
    unnamed x20 -> x9, local copies, waits for them, and re-layouts: 1.97 us -> 1.78 us
where the time goes in v3:
time: 52.5 us; the launch traced here: 51.8 us
  Pallas kernels  45.1 us (86%)
  local copies, waits for them, and re-layouts  6.66 us (13%)
    pallas_call x1, Pallas kernels, body(): pl.pallas_call(functools.partial(layer_kernel, (cols, nr, local_rows, wid...  45.1 us
    unnamed x9, local copies, waits for them, and re-layouts  1.78 us
    transpose x1, local copies, waits for them, and re-layouts, body(): pixels.transpose(1, 0, 2).reshape(height * chan, width)  1.38 us

profile of v3, /device:TPU:28, one launch (start us, length us, event | category | flops | bytes accessed | tf_op | source)
XLA Modules:
  0.0 51.8 jit_solution(17909877084822086955)
XLA Ops:
  0.0 0.0 copy-start.1
  0.0 0.0 copy-start
  0.0 0.0 copy-start.2
  0.0 0.0 copy-start.3
  0.0 1.4 %copy.16 = bf16[128,3,512]{2,1,0:T(4,128)(2,1)S(1)} copy(bf16[128,3,512]{2,0,1:T(8,128)(2,1)} %bitcast.9) | data formatting | bytes 786432 | tf_op jit(solution)/shard_map/transpose | solution.py:422
  1.4 0.3 reshape.6
  1.7 0.8 %pad.4.x_ref = bf16[416,512]{1,0:T(8,128)(2,1)} pad(bf16[384,512]{1,0:T(8,128)(2,1)S(1)} %reshape.6, bf16[]{:T(256)} %constant.2.clone.1), padding=16_16x0_0 | pad | bytes 819202 | tf_op jit(solution)/shard_map/jit(_pad)/pad | solution.py:421
  2.5 0.0 copy-done.1
  2.5 0.6 %broadcast_in_dim.21.conv_b_ref = f32[1,1664]{1,0:T(1,128)} reshape(f32[1664]{0:T(1024)S(1)} %copy-done.1) | data formatting | bytes 13312 | tf_op jit(solution)/shard_map/broadcast_in_dim | solution.py:484
  3.1 0.0 copy-done
  3.1 0.6 %broadcast_in_dim.22.gain_ref = f32[1,1536]{1,0:T(1,128)} reshape(f32[1536]{0:T(1024)S(1)} %copy-done) | data formatting | bytes 12288 | tf_op jit(solution)/shard_map/broadcast_in_dim | solution.py:484
  3.7 0.0 copy-done.2
  3.7 0.6 %broadcast_in_dim.24.patch_b_ref = f32[1,768]{1,0:T(1,128)} reshape(f32[768]{0:T(1024)S(1)} %copy-done.2) | data formatting | bytes 6144 | tf_op jit(solution)/shard_map/broadcast_in_dim | solution.py:484
  4.3 0.0 copy-done.3
  4.3 0.6 %broadcast_in_dim.25.norm_g_ref = f32[1,768]{1,0:T(1,128)} reshape(f32[768]{0:T(1024)S(1)} %copy-done.3) | data formatting | bytes 6144 | tf_op jit(solution)/shard_map/broadcast_in_dim | solution.py:484
  4.9 45.1 %shard_map.136 = bf16[256,768]{1,0:T(8,128)(2,1)} custom-call(bf16[416,512]{1,0:T(8,128)(2,1)} %pad.4.x_ref, bf16[24,72,768]{2,1,0:T(8,128)(2,1)} %bitcast.8, bf16[768,1664]{1,0:T(8,128)(2,1)} %mix_hbm.1, bf16[768,1536]{1,0:T(8,128)(2,1)} %gate_hbm.1, bf16[1536,768]{1,0:T(8,128)(2,1)} %out_hbm.1, bf16[24,768]{1,0:T(8,128)(2,1)} %bitcast.10, ...), custom_call_target="tpu_custom_call" | custom-call | tf_op jit(solution)/shard_map/pallas_call | solution.py:431
  50.0 1.8 %copy.18 = bf16[256,768]{1,0:T(8,128)(2,1)} copy(bf16[256,768]{1,0:T(8,128)(2,1)} %shard_map.136) | data formatting | bytes 786432
Async XLA Ops:
  0.0 2.5 %copy-start.1 = (f32[1664]{0:T(1024)S(1)}, f32[1664]{0:T(1024)}, u32[]{:S(2)}) copy-start(f32[1664]{0:T(1024)} %param.24) | copy-start | bytes 19972
  0.0 3.1 %copy-start = (f32[1536]{0:T(1024)S(1)}, f32[1536]{0:T(1024)}, u32[]{:S(2)}) copy-start(f32[1536]{0:T(1024)} %param.26) | copy-start | bytes 18436
  0.0 3.7 %copy-start.2 = (f32[768]{0:T(1024)S(1)}, f32[768]{0:T(1024)}, u32[]{:S(2)}) copy-start(f32[768]{0:T(1024)} %param.16) | copy-start | bytes 9220
  0.0 4.3 %copy-start.3 = (f32[768]{0:T(1024)S(1)}, f32[768]{0:T(1024)}, u32[]{:S(2)}) copy-start(f32[768]{0:T(1024)} %param.17) | copy-start | bytes 9220
